TPU v7x, 32 devices: a whole 2x2x4 slice. The times are simulated.
32 devices in a mesh: dp: 16 (over z, y, core), fsdp: 2 (over x).
Axes of the slice: x: 2, y: 2, z: 4, core: 2. Of those that a mesh axis runs over, the one named last changes fastest.
Arguments:
- inputs: bfloat16 [32768, 512], P(('dp', 'fsdp')), may hold values from -6 to 6
- documents: int32 [32, 1024], P(('dp', 'fsdp')), may hold values from 0 to 7, never falling along the last dimension, each value on 1 to 512 neighbouring positions
- first_gain: bfloat16 [512], P(('dp', 'fsdp')), may hold values from 0.5 to 1.5
- first_shift: bfloat16 [512], P(('dp', 'fsdp')), may hold values from -1.75 to 1.75
- attend_weight: bfloat16 [512, 1536], P(('dp', 'fsdp')), may hold values from -0.25 to 0.25
- position_table: bfloat16 [256], P(('dp', 'fsdp')), may hold values from -6 to 6
- output_weight: bfloat16 [512, 512], P(('dp', 'fsdp')), may hold values from -1.5 to 1.5
- output_shift: bfloat16 [512], P(('dp', 'fsdp')), may hold values from -1.75 to 1.75
- second_gain: bfloat16 [512], P(('dp', 'fsdp')), may hold values from 0.5 to 1.5
- second_shift: bfloat16 [512], P(('dp', 'fsdp')), may hold values from -1.75 to 1.75
- expand_weight: bfloat16 [512, 2048], P(('dp', 'fsdp')), may hold values from -0.25 to 0.25
- expand_shift: bfloat16 [2048], P(('dp', 'fsdp')), may hold values from -1.75 to 1.75
- reduce_weight: bfloat16 [2048, 512], P(('dp', 'fsdp')), may hold values from -0.125 to 0.125
- reduce_shift: bfloat16 [512], P(('dp', 'fsdp')), may hold values from -1.75 to 1.75
- cotangent: bfloat16 [32768, 512], P(('dp', 'fsdp')), may hold values from -6 to 6
Outputs:
- output: bfloat16 [32768, 512], P(('dp', 'fsdp'))
- input_grad: float32 [32768, 512], P(('dp', 'fsdp'))
- first_gain_grad: float32 [512], P(('dp', 'fsdp'))
- first_shift_grad: float32 [512], P(('dp', 'fsdp'))
- attend_weight_grad: float32 [512, 1536], P(('dp', 'fsdp'))
- position_table_grad: float32 [256], P(('dp', 'fsdp'))
- output_weight_grad: float32 [512, 512], P(('dp', 'fsdp'))
- output_shift_grad: float32 [512], P(('dp', 'fsdp'))
- second_gain_grad: float32 [512], P(('dp', 'fsdp'))
- second_shift_grad: float32 [512], P(('dp', 'fsdp'))
- expand_weight_grad: float32 [512, 2048], P(('dp', 'fsdp'))
- expand_shift_grad: float32 [2048], P(('dp', 'fsdp'))
- reduce_weight_grad: float32 [2048, 512], P(('dp', 'fsdp'))
- reduce_shift_grad: float32 [512], P(('dp', 'fsdp'))
Inputs may be any that keep to these rules, and one draw needn't show every extreme that they name: `documents`: in each row the document numbers never fall, every number up to 7 appears, no document has more than 512 tokens and one in each row has exactly that many.
All inputs are finite; a program needn't handle non-finite values.
Results may differ from a plain program's by a relative error of at most 0.02.
Values may be sent and summed in bfloat16 or wider, within the bound.
A program may use at most 256 MiB of HBM per device.

v0:
```python
import types

import jax
import jax.numpy as jnp
from jax import lax
from jax.experimental import pallas as pl
from jax.experimental.pallas import tpu as pltpu
from jax.sharding import PartitionSpec as P

D = 512
HEADS = 8
HEAD_DIM = 64
BUCKETS = 32
LONGEST = 512
TILE = 128
PAIRS = HEADS // 2
HALF = D // 2
BLOCK = 512
WIDE = 512
NEG = -1e30
eps = 1e-05
far_reach = 128

bf16 = jnp.bfloat16
f32 = jnp.float32
AXES = ("dp", "fsdp")


def iota(shape, dim):
    return lax.broadcasted_iota(jnp.int32, shape, dim)


def bucket_of(distance):
    exact_count = BUCKETS // 2
    counted = jnp.minimum(distance, exact_count)
    for level_j in range(1, exact_count):
        border = int(exact_count * (far_reach / exact_count) ** (level_j / exact_count))
        counted = counted + (distance >= border).astype(jnp.int32)
    return counted


def dot_nn(a, b):
    return lax.dot_general(a, b, (((1,), (0,)), ((), ())), preferred_element_type=f32)


def dot_nt(a, b):
    return lax.dot_general(a, b, (((1,), (1,)), ((), ())), preferred_element_type=f32)


def dot_tn(a, b):
    return lax.dot_general(a, b, (((0,), (0,)), ((), ())), preferred_element_type=f32)


def onehot(mask):
    return jnp.where(mask, 1.0, 0.0).astype(bf16)


def standardize(v):
    center = v - jnp.mean(v, axis=-1, keepdims=True)
    spread = jnp.mean(center * center, axis=-1, keepdims=True)
    rstd = lax.rsqrt(spread + eps)
    return center * rstd, rstd


def standardize_back(dx, xh, rstd):
    return rstd * (
        dx
        - jnp.mean(dx, axis=-1, keepdims=True)
        - xh * jnp.mean(dx * xh, axis=-1, keepdims=True)
    )


def gelu_parts(h):
    phi = 0.5 + 0.5 * lax.erf(h * 0.7071067811865476)
    return h * phi, phi + h * (0.3989422804014327 * jnp.exp(-0.5 * h * h))


def split_heads(t):
    top = iota(t.shape, 0) < HEAD_DIM
    zero = jnp.zeros_like(t)
    return jnp.concatenate([jnp.where(top, t, zero), jnp.where(top, zero, t)], axis=1)


def join_heads(t):
    n = t.shape[1] // 2
    return jnp.concatenate([t[:HEAD_DIM, :n], t[HEAD_DIM:, n:]], axis=0)


def unpack_small(r, n):
    packed = r.WH[0][:, 3 * HALF :]
    rows, lanes = iota((16 * n, D), 0), iota((16 * n, D), 1)
    per = D // n
    rep = onehot(iota((128, D), 1) % per == iota((128, D), 0))
    wide = dot_nn(packed, rep)
    wide = jnp.where(lanes // per == rows // 16, wide, 0.0)
    r.sm[...] = jnp.sum(wide.reshape(n, 16, D), axis=0)
    per = HEADS * BUCKETS // n
    group = BUCKETS // per
    pick = onehot(iota((n, 16 * n), 1) == 16 * iota((n, 16 * n), 0) + 7)
    bucket = bucket_of(iota((128, 256), 1))
    rep = onehot(bucket % per == iota((128, 256), 0))
    wide = dot_nn(dot_nn(pick, packed).astype(bf16), rep)
    bucket = bucket_of(iota((n, 256), 1))
    wide = jnp.where(bucket // per == iota((n, 256), 0) % group, wide, 0.0).astype(bf16)
    gather = onehot(iota((HEADS, n), 1) // group == iota((HEADS, n), 0))
    r.bd[...] = dot_nn(gather, wide)


def unpack_expand_shift(r, n):
    packed = r.WH[0][:, 3 * HALF :]
    ff = r.es.shape[1]
    per = ff // n
    pick = onehot(iota((n, 16 * n), 1) == 16 * iota((n, 16 * n), 0) + 6)
    rep = onehot(iota((128, ff), 1) % per == iota((128, ff), 0))
    wide = dot_nn(dot_nn(pick, packed).astype(bf16), rep)
    wide = jnp.where(iota((n, ff), 1) // per == iota((n, ff), 0), wide, 0.0)
    r.es[...] = jnp.broadcast_to(jnp.sum(wide, axis=0, keepdims=True), r.es.shape)


def pack_small_grads(r, n):
    rows, lanes = iota((16 * n, D), 0), iota((16 * n, D), 1)
    per = D // n
    wide = jnp.broadcast_to(r.smg[...][None], (n, 16, D)).reshape(16 * n, D)
    wide = jnp.where(lanes // per == rows // 16, wide, 0.0).astype(bf16)
    rep = onehot(iota((128, D), 1) % per == iota((128, D), 0))
    packed = dot_nt(wide, rep)
    ff = r.esg.shape[1]
    per = ff // n
    rep = onehot(iota((128, ff), 1) % per == iota((128, ff), 0))
    wide = jnp.broadcast_to(r.esg[0:1, :], (n, ff))
    wide = jnp.where(iota((n, ff), 1) // per == iota((n, ff), 0), wide, 0.0).astype(bf16)
    part = dot_nt(wide, rep).astype(bf16)
    place = onehot(iota((16 * n, n), 0) == 16 * iota((16 * n, n), 1) + 6)
    packed = packed + dot_nn(place, part)
    per = HEADS * BUCKETS // n
    group = BUCKETS // per
    spread = onehot(iota((n, HEADS), 0) // group == iota((n, HEADS), 1))
    wide = dot_nn(spread, r.tg[...].astype(bf16))
    wide = jnp.where(iota((n, 128), 1) // per == iota((n, 128), 0) % group, wide, 0.0)
    rep = onehot(iota((128, 128), 1) % per == iota((128, 128), 0))
    part = dot_nt(wide.astype(bf16), rep).astype(bf16)
    place = onehot(iota((16 * n, n), 0) == 16 * iota((16 * n, n), 1) + 7)
    return packed + dot_nn(place, part)


def over_rows(length, body, block=BLOCK, unroll=2):
    def rows(i, c):
        for u in range(unroll):
            body(pl.ds(pl.multiple_of((i * unroll + u) * block, block), block))
        return c

    lax.fori_loop(0, length // block // unroll, rows, 0)


def standardize_first(r):
    def rows(s):
        r.xh2[s, :] = standardize(r.x[s, :].astype(f32))[0]

    over_rows(r.x.shape[0], rows, 256, 1)


def norm_first(r):
    def rows(s):
        r.na[s, :] = (r.xh2[s, :] * r.sm[0:1, :] + r.sm[1:2, :]).astype(bf16)

    over_rows(r.x.shape[0], rows, 256, 1)


def masks(r):
    length = r.docs.shape[1]
    same = iota((128, length), 0) == r.docs[...]
    r.kd[...] = jnp.where(same, 1.0, 0.0).T.astype(bf16)
    differ = jnp.logical_and(iota((128, length), 0) < 8, jnp.logical_not(same))
    r.qd[...] = jnp.where(differ, NEG, 0.0).astype(bf16)


def near_bias(r):
    for h in range(HEADS):
        by_dist = r.bd[h : h + 1, :]
        by_dist = by_dist - by_dist[:, 255:256]
        line = jnp.concatenate([jnp.full((1, TILE), NEG, f32), by_dist], axis=1)
        line = jnp.broadcast_to(line, (TILE, 3 * TILE))
        line = pltpu.roll(line, 0, 1, stride=1, stride_axis=0)
        half = slice((h % 2) * TILE, (h % 2 + 1) * TILE)
        r.near[h // 2, 0:TILE, half] = line[:, 2 * TILE :]
        r.near[h // 2, TILE:, half] = line[:, TILE : 2 * TILE]


def project(r, half):
    def rows(s):
        out = dot_nn(r.na[s, :], r.WH[half][:, 0 : 3 * HALF])
        q = (out[:, :HALF].astype(bf16) * bf16(HEAD_DIM**-0.5)).T
        k = out[:, HALF : 2 * HALF].astype(bf16)
        v = out[:, 2 * HALF :].astype(bf16)
        for j in range(2):
            lanes = slice(j * 128, (j + 1) * 128)
            r.qt[2 * half + j, :, s] = q[lanes, :]
            r.k[2 * half + j, s, :] = k[:, lanes]
            r.v[2 * half + j, s, :] = v[:, lanes]

    over_rows(r.x.shape[0], rows)


def bands(length):
    first = 0
    for b in range(length // TILE):
        low = max(0, b - LONGEST // TILE)
        count = (b + 1 - low) * TILE
        yield b, slice(low * TILE, (b + 1) * TILE), slice(b * TILE, (b + 1) * TILE), first, count
        first += count


def band_rows(length):
    return sum(count for _, _, _, _, count in bands(length))


def attend_forward(r, p):
    near = r.near[p]
    lanes = pl.ds(pl.multiple_of(p * 128, 128), 128)
    plan = list(bands(r.x.shape[0]))

    def scores(b, ks, qs, first, count):
        qd = r.qd[:, qs]
        rhs = jnp.concatenate(
            [split_heads(r.qt[p, :, qs]), jnp.concatenate([qd, qd], axis=1)], axis=0
        )
        lhs = jnp.concatenate([r.k[p, ks, :], r.kd[ks, :]], axis=1)
        st = dot_nn(lhs, rhs)
        if count > 2 * TILE:
            return jnp.concatenate([st[: count - 2 * TILE], st[count - 2 * TILE :] + near], axis=0)
        return st + near[2 * TILE - count :]

    def soften(st, b, first, count):
        lifted = jnp.exp(st - jnp.max(st, axis=0, keepdims=True))
        inverse = 1.0 / jnp.sum(lifted, axis=0, keepdims=True)
        weights = lifted.astype(bf16)
        r.P[p, first : first + count, :] = weights
        r.inv[p, b : b + 1, :] = inverse
        return weights, inverse

    def attended(weights, inverse, ks, qs):
        ot = join_heads(dot_tn(r.v[p, ks, :], weights) * inverse)
        r.ot[p, :, qs] = ot
        r.att[qs, lanes] = ot.T.astype(bf16)

    AHEAD = 1
    queue, soft = [], []
    steps = len(plan)
    for i in range(steps + 2):
        if i < steps:
            queue.append(scores(*plan[i]))
        if 1 <= i <= steps:
            b, ks, qs, first, count = plan[i - 1]
            soft.append(soften(queue.pop(0), b, first, count))
        if 2 <= i:
            b, ks, qs, first, count = plan[i - 2]
            attended(*soft.pop(0), ks, qs)


def attend_backward(r, p):
    length = r.x.shape[0]
    r.dk[...] = jnp.zeros_like(r.dk)
    r.dv[...] = jnp.zeros_like(r.dv)
    r.acc[...] = jnp.zeros_like(r.acc)
    inner = pl.multiple_of((p // 2) * 3 * HALF + (p % 2) * 128, 128)
    top = iota((128, TILE), 0) < HEAD_DIM
    plan = list(bands(length))

    def soft_grad(b, ks, qs, first, count):
        inverse = r.inv[p, b : b + 1, :]
        scale = jnp.where(top, inverse[:, :TILE], inverse[:, TILE:])
        dot_ = (r.dot[p, :, qs].astype(f32) * scale).astype(bf16)
        prod = dot_.astype(f32) * r.ot[p, :, qs]
        delta = jnp.concatenate(
            [
                jnp.sum(prod[:HEAD_DIM], axis=0, keepdims=True),
                jnp.sum(prod[HEAD_DIM:], axis=0, keepdims=True),
            ],
            axis=1,
        )
        dcat = split_heads(dot_)
        return dcat, delta, dot_nn(r.v[p, ks, :], dcat)

    def score_grad(dcat, delta, dpt, first, count):
        weights = r.P[p, first : first + count, :]
        ds = weights.astype(f32) * (dpt - delta)
        if count >= 2 * TILE:
            r.acc[...] += ds[count - 2 * TILE :]
        else:
            r.acc[TILE:, :] += ds
        return weights, dcat, ds.astype(bf16)

    def operand_grads(weights, dcat, dsb, ks, qs):
        r.dv[ks, :] += dot_nt(weights, dcat)
        r.dk[ks, :] += dot_nt(dsb, split_heads(r.qt[p, :, qs]))
        dqt = join_heads(dot_tn(r.k[p, ks, :], dsb)) * HEAD_DIM**-0.5
        r.gh[qs, pl.ds(inner, 128)] = dqt.T.astype(bf16)

    soft, score = [], []
    steps = len(plan)
    for i in range(steps + 2):
        if i < steps:
            soft.append(soft_grad(*plan[i]))
        if 1 <= i <= steps:
            b, ks, qs, first, count = plan[i - 1]
            score.append(score_grad(*soft.pop(0), first, count))
        if 2 <= i:
            b, ks, qs, first, count = plan[i - 2]
            operand_grads(*score.pop(0), ks, qs)
    r.gh[:, pl.ds(HALF + inner, 128)] = r.dk[...].astype(bf16)
    r.gh[:, pl.ds(2 * HALF + inner, 128)] = r.dv[...].astype(bf16)
    zero = jnp.zeros((TILE, TILE), f32)
    rows = iota((TILE, 3 * TILE), 0)
    for h in range(2):
        half = slice(h * TILE, (h + 1) * TILE)
        line = jnp.concatenate([zero, r.acc[TILE:, half], r.acc[:TILE, half]], axis=1)
        for bit in range(7):
            rolled = pltpu.roll(line, 3 * TILE - (1 << bit), 1)
            line = jnp.where((rows >> bit) & 1 == 1, rolled, line)
        r.lines[pl.ds(2 * p + h, 1), :] = jnp.sum(line, axis=0, keepdims=True)


def table_grad(r):
    by_dist = r.lines[:, TILE:]
    dist = iota((2 * TILE, 128), 0)
    near = jnp.logical_and(bucket_of(dist) == iota((2 * TILE, 128), 1), dist < 2 * TILE)
    near = jnp.logical_and(near, iota((2 * TILE, 128), 1) < BUCKETS - 1)
    counted = lax.dot_general(
        by_dist,
        jnp.where(near, 1.0, 0.0),
        (((1,), (0,)), ((), ())),
        precision=lax.Precision.HIGHEST,
        preferred_element_type=f32,
    )
    rest = -jnp.sum(counted, axis=1, keepdims=True)
    r.tg[...] = jnp.where(iota((HEADS, 128), 1) == BUCKETS - 1, rest, counted)


def before_ff(r):
    r.smg[...] = jnp.zeros_like(r.smg)
    r.esg[...] = jnp.zeros_like(r.esg)

    def rows(s):
        residual = r.x[s, :].astype(f32) + dot_nn(r.att[s, :], r.WO[...]) + r.sm[2:3, :]
        xh, rstd = standardize(residual)
        r.xh2[s, :] = xh
        r.rstd2[s, :] = rstd
        r.nf[s, :] = (xh * r.sm[3:4, :] + r.sm[4:5, :]).astype(bf16)
        r.branch[s, :] = residual + r.sm[5:6, :]

    over_rows(r.x.shape[0], rows)


def feed_forward(r, f):
    cols = slice(f * WIDE, (f + 1) * WIDE)
    half = r.W1[f // 2]
    inner = slice((f % 2) * WIDE, (f % 2 + 1) * WIDE)

    def rows(s):
        hidden = dot_nn(r.nf[s, :], half[:, inner]) + r.es[0:1, cols]
        active, slope = gelu_parts(hidden)
        r.act[s, cols] = active.astype(bf16)
        r.gh[s, cols] = slope.astype(bf16)

    over_rows(r.x.shape[0], rows, 256, 4)


def feed_backward(r, f):
    cols = slice(f * WIDE, (f + 1) * WIDE)

    def rows(s):
        gh = dot_nt(r.g[s, :], r.W2[cols, :]) * r.gh[s, cols].astype(f32)
        r.esg[0:1, cols] += jnp.sum(gh, axis=0, keepdims=True)
        r.gh[s, cols] = gh.astype(bf16)

    over_rows(r.x.shape[0], rows)


def after_ff(r, s):
    ff = r.es.shape[1]
    gnf = dot_nt(r.gh[s, : ff // 2], r.W1[0][...]) + dot_nt(r.gh[s, ff // 2 :], r.W1[1][...])
    xh = r.xh2[s, :]
    gf = r.g[s, :].astype(f32)
    grad = gf + standardize_back(gnf * r.sm[3:4, :], xh, r.rstd2[s, :])
    r.xh2[s, :] = grad
    gb = grad.astype(bf16)
    r.gb[s, :] = gb
    r.smg[2:3, :] += jnp.sum(gb.astype(f32), axis=0, keepdims=True)
    r.smg[3:4, :] += jnp.sum(gnf * xh, axis=0, keepdims=True)
    r.smg[4:5, :] += jnp.sum(gnf, axis=0, keepdims=True)
    r.smg[5:6, :] += jnp.sum(gf, axis=0, keepdims=True)
    dot_ = dot_nt(gb, r.WO[...]).astype(bf16).T
    for p in range(PAIRS):
        r.dot[p, :, s] = dot_[p * 128 : (p + 1) * 128, :]


def output(r, s):
    r.nf[s, :] = (r.branch[s, :] + dot_nn(r.act[s, :], r.W2[...])).astype(bf16)


def half_columns(half):
    return slice(half * 3 * HALF, (half + 1) * 3 * HALF)


def pair_columns(ref, rows, p, base=0):
    at = base + (p % 2) * 128
    return jnp.concatenate(
        [ref[rows, part * HALF + at : part * HALF + at + 128] for part in range(3)], axis=1
    )


def back_project(r, half, pair=None):
    def rows(s):
        if pair is None:
            grads, weight = r.gh[s, half_columns(half)], r.WH[half][:, 0 : 3 * HALF]
        else:
            grads = pair_columns(r.gh, s, pair, half * 3 * HALF)
            weight = pair_columns(r.WH[half], slice(None), pair)
        part = dot_nt(grads, weight)
        r.gnf[s, :] = part if half == 0 else r.gnf[s, :] + part

    over_rows(r.x.shape[0], rows)


def last(r):
    def rows(s):
        gna = r.gnf[s, :]
        xh, rstd = standardize(r.x[s, :].astype(f32))
        r.xh2[s, :] += standardize_back(gna * r.sm[0:1, :], xh, rstd)
        r.smg[0:1, :] += jnp.sum(gna * xh, axis=0, keepdims=True)
        r.smg[1:2, :] += jnp.sum(gna, axis=0, keepdims=True)

    over_rows(r.x.shape[0], rows)


def weight_grad(left, right, step, put):
    count = left.shape[1] // step
    if count == 1:
        put(0, dot_tn(left[...], right()))
        return

    def rows(i, c):
        put(i, dot_tn(left[:, pl.ds(pl.multiple_of(i * step, step), step)], right()))
        return c

    lax.fori_loop(0, count, rows, 0)


class Place:
    def __init__(self, dp_size, fsdp_size):
        dp, x = lax.axis_index("dp"), lax.axis_index("fsdp")
        self.z, self.y, self.c, self.x = dp // 4, (dp // 2) % 2, dp % 2, x
        self.zs = dp_size // 4

    def zpeer(self, m):
        z = self.z
        return (z, z + 1 - 2 * (z % 2), (z + 2) % 4, 3 - z)[m]

    def index(self, m, t, other=False):
        x = 1 - self.x if t in (1, 3) else self.x
        y = 1 - self.y if t in (2, 3) else self.y
        c = 1 - self.c if other else self.c
        return ((self.zpeer(m) * 2 + y) * 2 + c) * 2 + x

    def inner(self, t, other=False):
        x = 1 - self.x if t in (1, 3) else self.x
        y = 1 - self.y if t in (2, 3) else self.y
        c = 1 - self.c if other else self.c
        return (y * 2 + c) * 2 + x

    def device(self, m=0, t=0, other=False):
        x = 1 - self.x if t in (1, 3) else self.x
        y = 1 - self.y if t in (2, 3) else self.y
        c = 1 - self.c if other else self.c
        return ((self.zpeer(m) * 2 + y) * 2 + c, x)

    def neighbours(self):
        return [self.device(m=m) for m in (1, 2, 3)] + [
            self.device(t=1),
            self.device(t=2),
            self.device(t=3),
            self.device(other=True),
        ]


def greet(place):
    barrier = pltpu.get_barrier_semaphore()
    for peer in place.neighbours():
        pl.semaphore_signal(
            barrier, inc=1, device_id=peer, device_id_type=pl.DeviceIdType.MESH
        )


def enter():
    pl.semaphore_wait(pltpu.get_barrier_semaphore(), 7)


GATHER_SEMS, SCATTER_SEMS = 8, 9
X, Y, OPPOSITE_A, OPPOSITE_B, SIBLING = 3, 4, 5, 6, 7


class Gather:
    def __init__(self, place, whole, rho, half, send, recv):
        self.place, self.whole, self.rho, self.half = place, whole, rho, half
        self.send, self.recv = send, recv

    def view(self, shard, part=None, count=1):
        rows = pl.ds(pl.multiple_of(shard * self.rho, 16), count * self.rho)
        if part is None:
            return self.whole.at[rows, :]
        cols = slice(0, self.half) if part == 0 else slice(self.half, self.whole.shape[1])
        return self.whole.at[rows, cols]

    def copy(self, ref, sem, device):
        return pltpu.make_async_remote_copy(
            src_ref=ref,
            dst_ref=ref,
            send_sem=self.send,
            recv_sem=self.recv.at[sem],
            device_id=device,
            device_id_type=pl.DeviceIdType.MESH,
        )

    def start(self, shard, sem, device, part=None):
        self.copy(self.view(shard, part), sem, device).start()

    def arrive(self, count, sem, part=None):
        ref = self.view(0, part, count)
        self.copy(ref, sem, self.place.device(other=True)).wait_recv()

    def along_z(self):
        at = self.place
        for m in (1, 2, 3):
            self.start(at.index(0, 0), m - 1, at.device(m=m))

    def first(self):
        self.along_z()
        self.spread(0)

    def spread(self, m):
        at = self.place
        shard = at.index(m, 0)
        self.start(shard, X, at.device(t=1))
        self.start(shard, Y, at.device(t=2))
        if self.half is None:
            self.start(shard, OPPOSITE_A, at.device(t=3))
        self.start(shard, SIBLING, at.device(other=True))

    def second(self):
        for m in (1, 2, 3):
            self.arrive(1, m - 1)
            self.spread(m)

    def third(self):
        at = self.place
        self.arrive(4, X)
        for m in range(4):
            if self.half is not None:
                self.start(at.index(m, 1), OPPOSITE_A, at.device(t=2), 0)
        for m in range(4):
            self.start(at.index(m, 1), SIBLING, at.device(other=True))
        self.arrive(4, Y)
        for m in range(4):
            if self.half is not None:
                self.start(at.index(m, 2), OPPOSITE_B, at.device(t=1), 1)
        for m in range(4):
            self.start(at.index(m, 2), SIBLING, at.device(other=True))

    def fourth(self):
        at = self.place
        if self.half is None:
            self.arrive(4, OPPOSITE_A)
        else:
            self.arrive(4, OPPOSITE_A, 0)
            self.arrive(4, OPPOSITE_B, 1)
        for m in range(4):
            self.start(at.index(m, 3), SIBLING, at.device(other=True))

    def finish(self):
        self.arrive(16, SIBLING)

    def drain(self):
        self.copy(self.view(0, None, 31), X, self.place.device(other=True)).wait_send()


class Scatter:
    def __init__(self, place, full, bufs, half, send, recv, emit):
        self.place, self.full, self.half, self.emit = place, full, half, emit
        self.sib, self.ra, self.rb, self.rx, self.ry, self.rz = bufs
        self.send, self.recv = send, recv

    def copy(self, src, dst, sem, device):
        group = 0 if sem < 4 else 1 if sem < 8 else 2
        return pltpu.make_async_remote_copy(
            src_ref=src,
            dst_ref=dst,
            send_sem=self.send.at[group],
            recv_sem=self.recv.at[sem],
            device_id=device,
            device_id_type=pl.DeviceIdType.MESH,
        )

    def start(self, src, dst, sem, device):
        self.copy(src, dst, sem, device).start()

    def arrive(self, dst, sem):
        self.copy(dst, dst, sem, self.place.device(other=True)).wait_recv()

    def first(self):
        at = self.place
        for t in (3, 1, 2, 0):
            self.start(
                self.full.at[:, at.inner(t, other=True)], self.sib.at[t], t, at.device(other=True)
            )

    def merge(self, t):
        self.arrive(self.sib.at[t], t)
        self.sib[t] += self.full[:, self.place.inner(t)]

    def second(self):
        at = self.place
        self.merge(3)
        if self.half is None:
            self.start(self.sib.at[3], self.ra, 4, at.device(t=3))
            self.merge(1)
            self.start(self.sib.at[1], self.rx, 6, at.device(t=1))
            self.merge(2)
            self.start(self.sib.at[2], self.ry, 7, at.device(t=2))
        else:
            self.start(self.sib.at[3, :, :, : self.half], self.ra, 4, at.device(t=1))
            self.start(self.sib.at[3, :, :, self.half :], self.rb, 5, at.device(t=2))

    def third(self):
        at = self.place
        if self.half is None:
            return
        self.merge(1)
        self.merge(2)
        self.arrive(self.rb, 5)
        self.sib[1, :, :, self.half :] += self.rb[...]
        self.start(self.sib.at[1], self.rx, 6, at.device(t=1))
        self.arrive(self.ra, 4)
        self.sib[2, :, :, : self.half] += self.ra[...]
        self.start(self.sib.at[2], self.ry, 7, at.device(t=2))

    def fourth(self):
        at = self.place
        self.merge(0)
        self.arrive(self.rx, 6)
        self.arrive(self.ry, 7)
        total = self.rx[...].astype(f32) + self.ry[...].astype(f32)
        if self.half is None:
            self.arrive(self.ra, 4)
            total = total + self.ra[...].astype(f32)
        self.sib[0] += total.astype(bf16)
        for m in (1, 2, 3):
            self.start(self.sib.at[0, at.zpeer(m)], self.rz.at[m - 1], 8, at.device(m=m))

    def fifth(self):
        self.arrive(self.rz, 8)
        total = self.sib[0, self.place.z].astype(f32)
        for m in (1, 2, 3):
            total = total + self.rz[m - 1].astype(f32)
        self.emit(total)

    def drain(self):
        for sem, ref in ((0, self.sib), (4, self.sib.at[0:3]), (8, self.rz)):
            self.copy(ref, ref, sem, self.place.device(other=True)).wait_send()


class ScatterByPlane(Scatter):
    def copy(self, src, dst, sem, device):
        group = 0 if sem < 16 else 1 if sem < 32 else 2
        return pltpu.make_async_remote_copy(
            src_ref=src,
            dst_ref=dst,
            send_sem=self.send.at[group],
            recv_sem=self.recv.at[sem],
            device_id=device,
            device_id_type=pl.DeviceIdType.MESH,
        )

    def first(self, z):
        at = self.place
        for t in (3, 1, 2, 0):
            self.start(
                self.full.at[z, at.inner(t, other=True)],
                self.sib.at[t, z],
                4 * t + z,
                at.device(other=True),
            )

    def merge(self, t, z):
        self.arrive(self.sib.at[t, z], 4 * t + z)
        self.sib[t, z] += self.full[z, self.place.inner(t)]

    def second(self, z):
        at = self.place
        self.merge(3, z)
        self.start(self.sib.at[3, z, :, : self.half], self.ra.at[z], 16 + z, at.device(t=1))
        self.start(self.sib.at[3, z, :, self.half :], self.rb.at[z], 20 + z, at.device(t=2))

    def third(self, z):
        at = self.place
        self.merge(1, z)
        self.merge(2, z)
        self.arrive(self.rb.at[z], 20 + z)
        self.sib[1, z, :, self.half :] += self.rb[z]
        self.start(self.sib.at[1, z], self.rx.at[z], 24 + z, at.device(t=1))
        self.arrive(self.ra.at[z], 16 + z)
        self.sib[2, z, :, : self.half] += self.ra[z]
        self.start(self.sib.at[2, z], self.ry.at[z], 28 + z, at.device(t=2))

    def fourth(self):
        at = self.place
        for z in range(4):
            self.merge(0, z)
            self.arrive(self.rx.at[z], 24 + z)
            self.arrive(self.ry.at[z], 28 + z)
            total = self.rx[z].astype(f32) + self.ry[z].astype(f32)
            self.sib[0, z] += total.astype(bf16)
        for m in (1, 2, 3):
            self.start(self.sib.at[0, at.zpeer(m)], self.rz.at[m - 1], 32, at.device(m=m))

    def fifth(self):
        self.arrive(self.rz, 32)
        total = self.sib[0, self.place.z].astype(f32)
        for m in (1, 2, 3):
            total = total + self.rz[m - 1].astype(f32)
        self.emit(total)

    def drain(self):
        for sem, ref in ((0, self.sib), (16, self.sib.at[0:3]), (32, self.rz)):
            self.copy(ref, ref, sem, self.place.device(other=True)).wait_send()


def scatter_bufs(rho, cols, half):
    first = cols if half is None else half
    rest = 128 if half is None else cols - half
    return [
        pltpu.VMEM((4, 4, rho, cols), bf16),
        pltpu.VMEM((4, rho, first), bf16),
        pltpu.VMEM((4, rho, rest), bf16),
        pltpu.VMEM((4, rho, cols), bf16),
        pltpu.VMEM((4, rho, cols), bf16),
        pltpu.VMEM((3, rho, cols), bf16),
    ]


def over_pairs(attend, r, first, end, pump):
    def one(p, c):
        attend(r, p)
        for pair in range(first, end):
            if pair in pump:

                @pl.when(p == pair)
                def _():
                    pump[pair]()
        return c

    lax.fori_loop(first, end, one, 0)


def work_scratch(length, ff):
    tokens = band_rows(length)
    return dict(
        x=pltpu.VMEM((length, D), bf16),
        na=pltpu.VMEM((length, D), bf16),
        kd=pltpu.VMEM((length, 128), bf16),
        qd=pltpu.VMEM((128, length), bf16),
        near=pltpu.VMEM((PAIRS, 2 * TILE, 2 * TILE), f32),
        qt=pltpu.VMEM((PAIRS, 128, length), bf16),
        k=pltpu.VMEM((PAIRS, length, 128), bf16),
        v=pltpu.VMEM((PAIRS, length, 128), bf16),
        P=pltpu.VMEM((PAIRS, tokens, 2 * TILE), bf16),
        inv=pltpu.VMEM((PAIRS, length // TILE, 2 * TILE), f32),
        ot=pltpu.VMEM((PAIRS, 128, length), f32),
        att=pltpu.VMEM((length, D), bf16),
        xh2=pltpu.VMEM((length, D), f32),
        rstd2=pltpu.VMEM((length, 1), f32),
        branch=pltpu.VMEM((length, D), f32),
        gnf=pltpu.VMEM((length, D), f32),
        nf=pltpu.VMEM((length, D), bf16),
        act=pltpu.VMEM((length, ff), bf16),
        gh=pltpu.VMEM((length, ff), bf16),
        gb=pltpu.VMEM((length, D), bf16),
        dot=pltpu.VMEM((PAIRS, 128, length), bf16),
        dk=pltpu.VMEM((length, 128), f32),
        dv=pltpu.VMEM((length, 128), f32),
        acc=pltpu.VMEM((2 * TILE, 2 * TILE), f32),
        lines=pltpu.VMEM((HEADS, 3 * TILE), f32),
    )


def small_scratch(ff):
    return dict(
        sm=pltpu.VMEM((16, D), f32),
        es=pltpu.VMEM((8, ff), f32),
        bd=pltpu.VMEM((HEADS, 256), f32),
        smg=pltpu.VMEM((16, D), f32),
        esg=pltpu.VMEM((8, ff), f32),
        tg=pltpu.VMEM((HEADS, 128), f32),
    )


def run_kernel(kernel, operands, out_shape, scratch, in_hbm=(), out_hbm=(), **params):
    names = list(scratch)
    count = len(operands) + len(out_shape)

    def named(*refs):
        kernel(refs[: len(operands)], refs[len(operands) : count], dict(zip(names, refs[count:])))

    def specs(number, hbm):
        return [
            pl.BlockSpec(memory_space=pl.ANY if i in hbm else pltpu.VMEM) for i in range(number)
        ]

    return pl.pallas_call(
        named,
        out_shape=out_shape,
        in_specs=specs(len(operands), in_hbm),
        out_specs=specs(len(out_shape), out_hbm),
        scratch_shapes=[scratch[name] for name in names],
        compiler_params=pltpu.CompilerParams(vmem_limit_bytes=VMEM_BYTES, **params),
    )(*operands)


VMEM_BYTES = 63 * 1024 * 1024


def whole_layer(x, documents, g, small, w_a, w_o, w_1, w_2, dp_size, fsdp_size):
    n = dp_size * fsdp_size
    length, ff = x.shape[0], w_1.shape[1]
    ra, r2 = w_1.shape[0], w_2.shape[0]
    gathered = dict(
        H0=(ra, 3 * HALF + 128, None),
        H1=(ra, 3 * HALF, None),
        WO=(ra, D, HALF),
        W2=(r2, D, HALF),
        W1a=(ra, ff // 2, ff // 4),
        W1b=(ra, ff // 2, ff // 4),
    )
    scattered = dict(
        d1a=(ra, ff // 2, ff // 4),
        d1b=(ra, ff // 2, ff // 4),
        d2=(r2, D, HALF),
        dO=(ra, D, HALF),
        dH=(ra, 3 * HALF, HALF),
        dT2=(ra, 384, 128),
        dT3=(ra, 384, None),
        dS=(ra, 128, None),
    )
    scratch = dict(work_scratch(length, ff), **small_scratch(ff))
    scratch["g"] = pltpu.VMEM((length, D), bf16)
    for name, (rho, cols, _) in gathered.items():
        scratch[name] = pltpu.VMEM((n * rho, cols), bf16)
    for name, (rho, cols, half) in scattered.items():
        scratch[name] = pltpu.VMEM((4, 8, rho, cols), bf16)
        for j, buf in enumerate(scatter_bufs(rho, cols, half)):
            scratch["%s_%d" % (name, j)] = buf
    dma = pltpu.SemaphoreType.DMA
    scratch.update(
        gsend=dma((len(gathered),)),
        grecv=dma((len(gathered), GATHER_SEMS)),
        prec=dma((33,)),
        ssend=dma((len(scattered), 3)),
        srecv=dma((len(scattered), SCATTER_SEMS)),
        move=dma((4,)),
    )

    def kernel(ins, outs, s):
        r = types.SimpleNamespace(**s)
        x_in, r.docs, g_in = ins[:3]
        vectors, (own_a, own_o, own_1, own_2) = ins[3:11], ins[11:]
        out, igrad, out_a, out_o, out_1, out_2, out_s = outs
        r.WH, r.W1 = [r.H0, r.H1], [r.W1a, r.W1b]
        at = Place(dp_size, fsdp_size)
        get_x = pltpu.make_async_copy(x_in, r.x, r.move.at[0])
        get_g = pltpu.make_async_copy(g_in, r.g, r.move.at[1])
        put_out = pltpu.make_async_copy(r.nf, out, r.move.at[2])
        put_igrad = pltpu.make_async_copy(r.xh2, igrad, r.move.at[3])
        get_x.start()
        get_g.start()
        greet(at)
        mine = at.index(0, 0)
        rows_a = pl.ds(pl.multiple_of(mine * ra, 16), ra)
        rows_2 = pl.ds(pl.multiple_of(mine * r2, 16), r2)
        for half, ref in enumerate(r.WH):
            for part in range(3):
                ref[rows_a, part * HALF : (part + 1) * HALF] = own_a[
                    :, part * D + half * HALF : part * D + (half + 1) * HALF
                ]
        lines = [
            jnp.concatenate(
                [v[...].astype(f32), jnp.zeros((1, 128 - v.shape[1]), f32)], axis=1
            )
            for v in vectors
        ]
        lines.append(jnp.zeros((ra - len(lines), 128), f32))
        r.H0[rows_a, 3 * HALF :] = jnp.concatenate(lines, axis=0).astype(bf16)
        r.WO[rows_a, :] = own_o[...]
        r.W2[rows_2, :] = own_2[...]
        for half, ref in enumerate(r.W1):
            ref[rows_a, :] = own_1[:, half * ff // 2 : (half + 1) * ff // 2]
        gathers = {
            name: Gather(at, s[name], rho, half, r.gsend.at[i], r.grecv.at[i])
            for i, (name, (rho, _, half)) in enumerate(gathered.items())
        }
        h0, h1, wo, w2, w1a, w1b = gathers.values()
        enter()
        h0.first()
        masks(r)
        get_x.wait()
        standardize_first(r)
        h0.second()
        h1.first()
        wo.first()
        h0.third()
        h0.fourth()
        h0.finish()
        unpack_small(r, n)
        norm_first(r)
        h1.second()
        w1a.first()
        near_bias(r)
        wo.second()
        project(r, 0)
        w1b.first()
        h1.third()
        w1a.second()

        def pump_0():
            h1.fourth()
            wo.third()
            w2.first()

        def pump_1():
            w1a.third()
            w1b.second()
            h1.finish()

        def pump_2():
            wo.fourth()
            w2.second()

        def pump_3():
            w1a.fourth()
            w1b.third()
            wo.finish()

        over_pairs(attend_forward, r, 0, 2, {0: pump_0, 1: pump_1})
        project(r, 1)
        over_pairs(attend_forward, r, 2, 4, {2: pump_2, 3: pump_3})
        unpack_expand_shift(r, n)
        before_ff(r)
        w1a.finish()
        get_g.wait()

        def emit_into(ref, cols):
            def emit(total):
                ref[:, cols] = total

            return emit

        def emit_pairs(pairs):
            def emit(total):
                wide = 128 * len(pairs)
                for part in range(3):
                    first = part * D + pairs[0] * 128
                    out_a[:, first : first + wide] = total[:, part * wide : (part + 1) * wide]

            return emit

        emits = dict(
            d1a=emit_into(out_1, slice(0, ff // 2)),
            d1b=emit_into(out_1, slice(ff // 2, ff)),
            d2=emit_into(out_2, slice(None)),
            dO=emit_into(out_o, slice(None)),
            dH=emit_pairs((0, 1)),
            dT2=emit_pairs((2,)),
            dT3=emit_pairs((3,)),
            dS=emit_into(out_s, slice(None)),
        )
        scatters = {
            name: (ScatterByPlane if name == "d2" else Scatter)(
                at,
                s[name],
                [s["%s_%d" % (name, j)] for j in range(6)],
                half,
                r.ssend.at[i],
                r.prec if name == "d2" else r.srecv.at[i],
                emits[name],
            )
            for i, (name, (_, _, half)) in enumerate(scattered.items())
        }
        s1a, s1b, s2, so, sh, st2, st3, ss = scatters.values()

        def put_shards(ref, step, rho, first=0):
            count = step // (8 * rho)

            def put(i, value):
                value = value.astype(bf16).reshape(count, 8, rho, value.shape[1])
                ref[pl.ds(count * i, count), :, :, first : first + value.shape[3]] = value

            return put

        def expand_grad(f, ref):
            cols = slice(f * WIDE, (f + 1) * WIDE)
            weight_grad(
                r.nf, lambda: r.gh[:, cols], D, put_shards(ref, D, ra, (f % 2) * WIDE)
            )

        def reduce_grad(f):
            act = r.act[:, f * WIDE : (f + 1) * WIDE]
            r.d2[f] = dot_tn(act, r.g[...]).astype(bf16).reshape(8, r2, D)
            s2.first(f)

        feed_forward(r, 0)
        reduce_grad(0)
        w1b.fourth()
        feed_forward(r, 1)
        reduce_grad(1)
        s2.second(0)
        w1b.finish()
        w2.third()
        feed_forward(r, 2)
        reduce_grad(2)
        s2.second(1)
        feed_forward(r, 3)
        reduce_grad(3)
        s2.third(0)
        s2.second(2)
        w2.fourth()
        s2.third(1)
        w2.finish()
        feed_backward(r, 0)
        expand_grad(0, r.d1a)
        s2.second(3)
        feed_backward(r, 1)
        expand_grad(1, r.d1a)
        s1a.first()
        s2.third(2)
        feed_backward(r, 2)
        expand_grad(2, r.d1b)
        s2.third(3)
        feed_backward(r, 3)
        expand_grad(3, r.d1b)
        s1b.first()
        s1a.second()
        after_ff(r, slice(0, BLOCK))
        s2.fourth()
        for i in range(1, length // BLOCK):
            after_ff(r, slice(i * BLOCK, (i + 1) * BLOCK))
        s1b.second()
        s1a.third()
        weight_grad(r.att, lambda: r.gb[...], D, put_shards(r.dO, D, ra))
        so.first()

        def pump_0():
            so.second()
            s1b.third()

        def pump_1():
            s2.fifth()
            s1a.fourth()
            so.third()

        def pump_2():
            sh.second()
            s1b.fourth()
            so.fourth()

        def pump_3():
            st2.second()
            sh.third()
            s1a.fifth()

        pump = {0: pump_0, 1: pump_1, 2: pump_2, 3: pump_3}
        over_pairs(attend_backward, r, 0, 2, pump)
        weight_grad(
            r.na, lambda: r.gh[:, half_columns(0)], D, put_shards(r.dH, D, ra)
        )
        sh.first()
        back_project(r, 0)
        over_pairs(attend_backward, r, 2, 3, pump)
        weight_grad(
            r.na, lambda: pair_columns(r.gh, slice(None), 2, 3 * HALF), D, put_shards(r.dT2, D, ra)
        )
        st2.first()
        back_project(r, 1, 2)
        over_pairs(attend_backward, r, 3, 4, pump)
        weight_grad(
            r.na, lambda: pair_columns(r.gh, slice(None), 3, 3 * HALF), D, put_shards(r.dT3, D, ra)
        )
        st3.first()
        back_project(r, 1, 3)
        last(r)
        put_igrad.start()
        st3.second()
        table_grad(r)
        r.dS[...] = pack_small_grads(r, n).astype(bf16).reshape(4, 8, ra, 128)
        ss.first()
        sh.fourth()
        st2.third()
        output(r, slice(0, BLOCK))
        ss.second()
        for i in range(1, length // BLOCK):
            output(r, slice(i * BLOCK, (i + 1) * BLOCK))
        put_out.start()
        s1b.fifth()
        so.fifth()
        st3.fourth()
        st2.fourth()
        ss.fourth()
        sh.fifth()
        st3.fifth()
        st2.fifth()
        ss.fifth()
        for item in list(gathers.values()) + list(scatters.values()):
            item.drain()
        put_out.wait()
        put_igrad.wait()

    out_shape = [
        jax.ShapeDtypeStruct((length, D), bf16),
        jax.ShapeDtypeStruct((length, D), f32),
        jax.ShapeDtypeStruct((ra, 3 * D), f32),
        jax.ShapeDtypeStruct((ra, D), f32),
        jax.ShapeDtypeStruct((ra, ff), f32),
        jax.ShapeDtypeStruct((r2, D), f32),
        jax.ShapeDtypeStruct((ra, 128), f32),
    ]
    operands = [x, documents, g, *small, w_a, w_o, w_1, w_2]
    return run_kernel(
        kernel,
        operands,
        out_shape,
        scratch,
        in_hbm=(0, 2),
        out_hbm=(0, 1),
        collective_id=0,
        has_side_effects=True,
    )


def hand_out(results, sizes):
    length = results[0].shape[0]
    pieces = 4
    chunk = length // pieces

    def kernel(ins, outs, s):
        buffers = (s["a"], s["b"])

        def move(i, j, back):
            rows = slice(j * chunk, (j + 1) * chunk)
            here = buffers[i].at[rows, :]
            there = (outs if back else ins)[i].at[rows, :]
            sem = s["move"].at[pieces * i + j, int(back)]
            if back:
                return pltpu.make_async_copy(here, there, sem)
            return pltpu.make_async_copy(there, here, sem)

        parts = [(i, j) for j in range(pieces) for i in range(2)]
        for i, j in parts:
            move(i, j, False).start()
        for i in range(2, 6):
            outs[i][...] = ins[i][...]
        for i, size in enumerate(sizes):
            outs[6 + i][...] = ins[6][i : i + 1, :size]
        for i, j in parts:
            move(i, j, False).wait()
            move(i, j, True).start()
        for i, j in parts:
            move(i, j, True).wait()

    out_shape = [jax.ShapeDtypeStruct(v.shape, v.dtype) for v in results[:6]]
    out_shape += [jax.ShapeDtypeStruct((1, size), f32) for size in sizes]
    scratch = dict(
        a=pltpu.VMEM(results[0].shape, results[0].dtype),
        b=pltpu.VMEM(results[1].shape, results[1].dtype),
        move=pltpu.SemaphoreType.DMA((2 * pieces, 2)),
    )
    return run_kernel(
        kernel, list(results), out_shape, scratch, in_hbm=(0, 1), out_hbm=(0, 1)
    )


def local_layer(x, documents, g, h0, h1, w_o, w_1a, w_1b, w_2, sm, es, bd):
    length, ff = x.shape[0], 2 * w_1a.shape[1]
    scratch = dict(work_scratch(length, ff))

    def kernel(ins, outs, s):
        r = types.SimpleNamespace(**s)
        x_in, r.docs, r.g, h0_, h1_, r.WO, w1a_, w1b_, r.W2, r.sm, r.es, r.bd = ins
        out, igrad, d_a, d_o, d_1, d_2, r.smg, r.esg, r.tg = outs
        r.WH, r.W1 = [h0_, h1_], [w1a_, w1b_]
        r.x[...] = x_in[...]
        masks(r)
        near_bias(r)
        standardize_first(r)
        norm_first(r)
        project(r, 0)
        project(r, 1)

        over_pairs(attend_forward, r, 0, PAIRS, {})
        before_ff(r)

        def put_into(ref, step, first, wide):
            def put(i, value):
                rows = pl.ds(pl.multiple_of(i * step, step), step)
                ref[rows, first : first + wide] = value.astype(ref.dtype)

            return put

        for f in range(ff // WIDE):
            feed_forward(r, f)
        weight_grad(r.act, lambda: r.g[...], 1024, put_into(d_2, 1024, 0, D))
        for f in range(ff // WIDE):
            cols = slice(f * WIDE, (f + 1) * WIDE)
            feed_backward(r, f)
            weight_grad(
                r.nf, lambda cols=cols: r.gh[:, cols], D, put_into(d_1, D, f * WIDE, WIDE)
            )
        for i in range(length // BLOCK):
            after_ff(r, slice(i * BLOCK, (i + 1) * BLOCK))
        for i in range(length // BLOCK):
            output(r, slice(i * BLOCK, (i + 1) * BLOCK))
        out[...] = r.nf[...]
        weight_grad(r.att, lambda: r.gb[...], D, put_into(d_o, D, 0, D))
        over_pairs(attend_backward, r, 0, PAIRS, {})
        for half in range(2):
            back_project(r, half)

            def put(i, value, half=half):
                for part in range(3):
                    first = part * D + half * HALF
                    d_a[:, first : first + HALF] = value[
                        :, part * HALF : (part + 1) * HALF
                    ].astype(bf16)

            weight_grad(r.na, lambda half=half: r.gh[:, half_columns(half)], D, put)
        last(r)
        table_grad(r)
        igrad[...] = r.xh2[...]

    out_shape = [
        jax.ShapeDtypeStruct((length, D), bf16),
        jax.ShapeDtypeStruct((length, D), f32),
        jax.ShapeDtypeStruct((D, 3 * D), bf16),
        jax.ShapeDtypeStruct((D, D), bf16),
        jax.ShapeDtypeStruct((D, ff), bf16),
        jax.ShapeDtypeStruct((ff, D), bf16),
        jax.ShapeDtypeStruct((16, D), f32),
        jax.ShapeDtypeStruct((8, ff), f32),
        jax.ShapeDtypeStruct((HEADS, 128), f32),
    ]
    operands = [x, documents, g, h0, h1, w_o, w_1a, w_1b, w_2, sm, es, bd]
    return run_kernel(kernel, operands, out_shape, scratch)


def whole_body(dp_size, fsdp_size):
    def body(x, documents, fg, fs, w_a, table, w_o, os, sg, ss, w_1, es, w_2, rs, g):
        vectors = (fg, fs, os, sg, ss, rs, es, table)
        results = whole_layer(
            x,
            documents,
            g,
            [v.reshape(1, -1) for v in vectors],
            w_a,
            w_o,
            w_1,
            w_2,
            dp_size,
            fsdp_size,
        )
        out, igrad, d_a, d_o, d_1, d_2, *small = hand_out(
            results, [v.shape[0] for v in vectors]
        )
        dfg, dfs, dos, dsg, dss, drs, des, dtable = [v.reshape(-1) for v in small]
        return (out, igrad, dfg, dfs, d_a, dtable, d_o, dos, dsg, dss, d_1, des, d_2, drs)

    return body


def split_body(x, documents, fg, fs, w_a, table, w_o, os, sg, ss, w_1, es, w_2, rs, g):
    def whole(v):
        return lax.all_gather(v, AXES, axis=0, tiled=True)

    def mine(v):
        return lax.psum_scatter(v.astype(f32), AXES, scatter_dimension=0, tiled=True)

    parts = [w_a[:, i * HALF : (i + 1) * HALF] for i in range(6)]
    h0 = whole(jnp.concatenate(parts[0::2], axis=1))
    h1 = whole(jnp.concatenate(parts[1::2], axis=1))
    ff = w_1.shape[1]
    rows = [whole(v).astype(f32) for v in (fg, fs, os, sg, ss, rs)]
    sm = jnp.concatenate([jnp.stack(rows), jnp.zeros((10, D), f32)], axis=0)
    wide = jnp.tile(whole(es).astype(f32)[None], (8, 1))
    bias = whole(table).astype(f32).reshape(HEADS, BUCKETS)
    bd = bias[:, bucket_of(jnp.arange(256, dtype=jnp.int32))]
    w_1 = whole(w_1)
    out, igrad, d_a, d_o, d_1, d_2, smg, esg, tg = local_layer(
        x,
        documents,
        g,
        h0,
        h1,
        whole(w_o),
        w_1[:, : ff // 2],
        w_1[:, ff // 2 :],
        whole(w_2),
        sm,
        wide,
        bd,
    )
    return (
        out,
        igrad,
        mine(smg[0]),
        mine(smg[1]),
        mine(d_a),
        mine(tg[:, :BUCKETS].reshape(HEADS * BUCKETS)),
        mine(d_o),
        mine(smg[2]),
        mine(smg[3]),
        mine(smg[4]),
        mine(d_1),
        mine(esg[0]),
        mine(d_2),
        mine(smg[5]),
    )


def solution(mesh):
    rows, flat = P(AXES, None), P(AXES)
    dp_size, fsdp_size = mesh.shape["dp"], mesh.shape["fsdp"]
    one_kernel = (dp_size, fsdp_size) == (16, 2)
    return jax.shard_map(
        whole_body(dp_size, fsdp_size) if one_kernel else split_body,
        mesh=mesh,
        in_specs=(
            rows,
            rows,
            flat,
            flat,
            rows,
            flat,
            rows,
            flat,
            flat,
            flat,
            rows,
            flat,
            rows,
            flat,
            rows,
        ),
        out_specs=(rows, rows, flat, flat, rows, flat, rows, flat, flat, flat, rows, flat, rows, flat),
        check_vma=False,
    )
```

profile of v0, /device:TPU:0, one launch (start us, length us, event | category | flops | bytes accessed | tf_op | source)
XLA Modules:
  0.0 107.0 jit_solution(5630385743005743696)
XLA Ops:
  0.7 101.5 %shard_map.254 = (bf16[1024,512]{1,0:T(8,128)(2,1)}, f32[1024,512]{1,0:T(8,128)}, f32[16,1536]{1,0:T(8,128)}, f32[16,512]{1,0:T(8,128)}, f32[16,2048]{1,0:T(8,12...) custom-call(bf16[1024,512]{1,0:T(8,128)(2,1)} %refs_0_.1, s32[1,1024]{1,0:T(1,128)} %refs_1_.1, bf16[1024,512]{1,0:T(8,128)(2,1)} %refs_2_.1, ...), custom_call_target="tpu_custom_call" | custom-call | tf_op jit(solution)/shard_map/pallas_call | solution.py:818
  102.2 4.7 %shard_map.255 = (bf16[1024,512]{1,0:T(8,128)(2,1)}, f32[1024,512]{1,0:T(8,128)}, f32[16,1536]{1,0:T(8,128)}, f32[16,512]{1,0:T(8,128)}, f32[16,2048]{1,0:T(8,12...) custom-call(bf16[1024,512]{1,0:T(8,128)(2,1)} %get-tuple-element.35., ...), custom_call_target="tpu_custom_call" | custom-call | tf_op jit(solution)/shard_map/pallas_call | solution.py:818
where the time goes:
time: 106 us; the launch traced here: 107 us
  Pallas kernels  106 us (100%)
    pallas_call x2, Pallas kernels, run_kernel(): pl.pallas_call(named, out_shape=out_shape, in_specs=specs(len(operands),...  106 us

commit v1 on v0

--- a/solution.py
+++ b/solution.py
@@ -846,7 +846,7 @@
         d2=(r2, D, HALF),
         dO=(ra, D, HALF),
         dH=(ra, 3 * HALF, HALF),
-        dT2=(ra, 384, 128),
+        dT2=(ra, 384, None),
         dT3=(ra, 384, None),
         dS=(ra, 128, None),
     )
@@ -1100,21 +1100,20 @@
         table_grad(r)
         r.dS[...] = pack_small_grads(r, n).astype(bf16).reshape(4, 8, ra, 128)
         ss.first()
-        sh.fourth()
-        st2.third()
         output(r, slice(0, BLOCK))
         ss.second()
+        sh.fourth()
+        st2.fourth()
         for i in range(1, length // BLOCK):
             output(r, slice(i * BLOCK, (i + 1) * BLOCK))
         put_out.start()
         s1b.fifth()
         so.fifth()
         st3.fourth()
-        st2.fourth()
         ss.fourth()
         sh.fifth()
+        st2.fifth()
         st3.fifth()
-        st2.fifth()
         ss.fifth()
         for item in list(gathers.values()) + list(scatters.values()):
             item.drain()

time: 106 us -> 106 us (level)
  no operation moved by 1% of the time
where the time goes in v1:
time: 106 us; the launch traced here: 107 us
  Pallas kernels  106 us (100%)
    pallas_call x2, Pallas kernels, run_kernel(): pl.pallas_call(named, out_shape=out_shape, in_specs=specs(len(operands),...  106 us

profile of v1, /device:TPU:0, one launch (start us, length us, event | category | flops | bytes accessed | tf_op | source)
XLA Modules:
  0.0 107.3 jit_solution(2702714628019625879)
XLA Ops:
  0.7 101.8 %shard_map.254 = (bf16[1024,512]{1,0:T(8,128)(2,1)}, f32[1024,512]{1,0:T(8,128)}, f32[16,1536]{1,0:T(8,128)}, f32[16,512]{1,0:T(8,128)}, f32[16,2048]{1,0:T(8,12...) custom-call(bf16[1024,512]{1,0:T(8,128)(2,1)} %refs_0_.1, s32[1,1024]{1,0:T(1,128)} %refs_1_.1, bf16[1024,512]{1,0:T(8,128)(2,1)} %refs_2_.1, ...), custom_call_target="tpu_custom_call" | custom-call | tf_op jit(solution)/shard_map/pallas_call | solution.py:818
  102.4 4.7 %shard_map.255 = (bf16[1024,512]{1,0:T(8,128)(2,1)}, f32[1024,512]{1,0:T(8,128)}, f32[16,1536]{1,0:T(8,128)}, f32[16,512]{1,0:T(8,128)}, f32[16,2048]{1,0:T(8,12...) custom-call(bf16[1024,512]{1,0:T(8,128)(2,1)} %get-tuple-element.35., ...), custom_call_target="tpu_custom_call" | custom-call | tf_op jit(solution)/shard_map/pallas_call | solution.py:818
